TPU v7x, 32 devices: a whole 2x2x4 slice. The times are simulated.
32 devices in a mesh: box: 8 (over z, core), dir: 4 (over y, x).
Axes of the slice: x: 2, y: 2, z: 4, core: 2. Of those that a mesh axis runs over, the one named last changes fastest.
Arguments:
- fine_density: bfloat16 [1024, 1536], P(('box', 'dir')), may hold values from -6 to 6
- coarse_density: bfloat16 [512, 3072], P(('box', 'dir')), may hold values from -6 to 6
- fine_operators: bfloat16 [192, 3072], replicated, may hold values from -0.109375 to 0.109375
- coarse_operators: bfloat16 [192, 3072], replicated, may hold values from -0.109375 to 0.109375
- fine_balance: int32 [8], replicated, may hold values from 0 to 7, each once
- coarse_balance: int32 [16], replicated, may hold values from 0 to 15, each once
- fine_sources: int32 [8, 16384], P('dir', 'box'), may hold values from 0 to 1023, as said below
- fine_targets: int32 [8, 16384], P('dir', 'box'), may hold values from 0 to 1023, as said below
- fine_op_ids: int32 [8, 16384], P('dir', 'box'), may hold values from 0 to 15
- coarse_sources: int32 [16, 8192], P('dir', 'box'), may hold values from 0 to 511, as said below
- coarse_targets: int32 [16, 8192], P('dir', 'box'), may hold values from 0 to 511, as said below
- coarse_op_ids: int32 [16, 8192], P('dir', 'box'), may hold values from 0 to 15
Outputs:
- fine_local: bfloat16 [1024, 1536], P('box', 'dir')
- coarse_local: bfloat16 [512, 3072], P('box', 'dir')
Inputs may be any that keep to these rules, and one draw needn't show every extreme that they name: `fine_targets`: pair column p belongs to the Morton range r = p // 2048; its target box lies in boxes r * 128 to (r + 1) * 128 - 1, and the first and last box of every range are named. `fine_sources`: the source of a pair of range r lies in boxes r * 128 - 32 to (r + 1) * 128 + 31, within the grid; in every range the sources at both ends of that span, as far as they lie in the grid, are named. `coarse_targets`: pair column p belongs to the Morton range r = p // 1024; its target box lies in boxes r * 64 to (r + 1) * 64 - 1, and the first and last box of every range are named. `coarse_sources`: the source of a pair of range r lies in boxes r * 64 - 32 to (r + 1) * 64 + 31, within the grid; in every range the sources at both ends of that span, as far as they lie in the grid, are named.
All inputs are finite; a program needn't handle non-finite values.
Results may differ from a plain program's by a relative error of at most 0.001.
Values may be sent and summed in bfloat16 or wider, within the bound.
A program may use at most 64 MiB of HBM per device.

v0:
```python
import functools

import jax
import jax.numpy as jnp
from jax import lax
from jax.experimental import pallas as pl
from jax.experimental.pallas import tpu as pltpu
from jax.sharding import PartitionSpec as P

RIM = 32
LANES = 128
BF16 = jnp.bfloat16
F32 = jnp.float32
MESH = pl.DeviceIdType.MESH


class Level:
    def __init__(self, density, operators, sources, nd):
        self.rows, width = density.shape
        self.channel = operators.shape[0]
        self.ops = operators.shape[1] // self.channel
        self.wedges = width // self.channel
        self.slots = self.wedges // nd
        self.targets = self.rows * nd
        self.halo = RIM // self.rows
        self.chunks = nd + 2 * self.halo
        self.span = self.targets + 2 * RIM
        self.pairs = sources.shape[1]
        self.full = self.span // LANES * LANES
        self.rest = self.span - self.full
        self.lo = 4 if self.rest else 2
        self.hi = self.ops // self.lo
        self.left = self.hi * self.targets
        self.right = self.lo * self.span
        self.depth = self.full + 2 * self.rest
        self.wide = -(-self.channel // LANES) * LANES


def one_hot(out, at, key, count):
    row = lax.broadcasted_iota(jnp.int32, (LANES, key.shape[1]), 0).astype(F32).astype(BF16)
    for base in range(0, count, LANES):
        near = (key - base).astype(F32).astype(BF16)
        hot = jnp.where(near == row, jnp.ones((), BF16), jnp.zeros((), BF16))
        out[base : base + LANES, :] = hot


def sort_slots(lv, nd, density, balance, split, send):
    for w in range(lv.wedges):
        split[w] = density[:, w * lv.channel : (w + 1) * lv.channel]
    for d in range(nd):
        parts = [split[balance[d * lv.slots + k]] for k in range(lv.slots)]
        send[d] = jnp.concatenate(parts, axis=1)


def copies(lv, nd, nb, b, d, send, ext, sems):
    send_sem, recv_sem = sems

    def copy(to_box, to_dir, chunk, sem):
        return pltpu.make_async_remote_copy(
            src_ref=send.at[to_dir],
            dst_ref=ext.at[chunk],
            send_sem=send_sem.at[sem],
            recv_sem=recv_sem.at[chunk],
            device_id=(to_box, to_dir),
            device_id_type=MESH,
        )

    sends, receives = [], []
    for step in range(nd):
        to = lax.rem(d + step, nd)
        up = jnp.logical_and(d >= nd - lv.halo, b < nb - 1)
        down = jnp.logical_and(d < lv.halo, b > 0)
        if step:
            sends.append((None, functools.partial(copy, b, to, lv.halo + d, step)))
        sends.append((up, functools.partial(copy, b + 1, to, d - (nd - lv.halo), nd + step)))
        sends.append((down, functools.partial(copy, b - 1, to, lv.halo + nd + d, 2 * nd + step)))
    for step in range(1, nd):
        chunk = lv.halo + lax.rem(d + step, nd)
        receives.append((None, functools.partial(copy, b, d, chunk, 0)))
    for i in range(lv.halo):
        receives.append((b > 0, functools.partial(copy, b, d, i, 0)))
        receives.append((b < nb - 1, functools.partial(copy, b, d, lv.halo + nd + i, 0)))
    return sends, receives


def under(condition, act):
    if condition is None:
        act()
    else:
        pl.when(condition)(act)


def histogram(lv, b, sources, targets, op_ids, left, right, counts):
    def body(j, _):
        at = pl.ds(j, 1)
        op = op_ids[at, :]
        high, low = op // lv.lo, op % lv.lo
        source = sources[at, :] - (b * lv.targets - RIM)
        target = targets[at, :] - b * lv.targets
        key = low * lv.full + source
        if lv.rest:
            tail = lv.lo * lv.full + low * lv.rest + (source - lv.full)
            key = jnp.where(source < lv.full, key, tail)
        one_hot(left, None, high * lv.targets + target, lv.left)
        one_hot(right, None, key, lv.right)
        found = lax.dot_general(
            left[...], right[...], (((1,), (1,)), ((), ())), preferred_element_type=F32
        )
        main = found.astype(BF16)
        counts[j, 0] = main
        counts[j, 1] = (found - main.astype(F32)).astype(BF16)
        return 0

    lax.fori_loop(0, lv.slots, body, 0)


def gather_rows(lv, ext, flat, weights):
    for q in range(lv.chunks):
        flat[q * lv.rows : (q + 1) * lv.rows, :] = ext[q].astype(flat.dtype)
    for j in range(lv.slots):
        mine = flat[:, j * lv.channel : (j + 1) * lv.channel].astype(BF16)
        pad = jnp.zeros((lv.span, lv.wide - lv.channel), BF16)
        mine = jnp.concatenate([mine, pad], axis=1)
        if lv.rest:
            none = jnp.zeros((lv.rest, lv.wide), BF16)
            weights[j, 0] = jnp.concatenate([mine, none], axis=0)
            weights[j, 1] = jnp.concatenate([mine[: lv.full], none, mine[lv.full :]], axis=0)
        else:
            weights[j, 0] = mine


def expand(lv, counts, weights, grown):
    def body(j, _):
        for low in range(lv.lo):
            picked = []
            for term in range(2):
                for k in range(lv.full // LANES):
                    first = low * lv.full + k * LANES
                    picked.append(counts[j, term, :, first : first + LANES])
                if lv.rest:
                    first = lv.lo * lv.full + (low // 2) * LANES
                    picked.append(counts[j, term, :, first : first + LANES])
            weight = weights[j, low % 2 if lv.rest else 0]
            total = jnp.dot(
                jnp.concatenate(picked, axis=1),
                jnp.concatenate([weight, weight], axis=0),
                preferred_element_type=F32,
            )
            main = total.astype(BF16)
            rest = (total - main.astype(F32)).astype(BF16)
            for high in range(lv.hi):
                op = high * lv.lo + low
                column = op // 2 * lv.wide
                rows = slice(high * lv.targets, (high + 1) * lv.targets)
                grown[op % 2, j, : lv.targets, column : column + lv.wide] = main[rows]
                grown[op % 2, j, lv.targets :, column : column + lv.wide] = rest[rows]
        return 0

    lax.fori_loop(0, lv.slots, body, 0)


def apply_operators(lv, grown, table, out):
    height = lv.slots * 2 * lv.targets
    total = []
    for parity in range(2):
        total.append(
            jnp.dot(
                grown[parity].reshape(height, grown.shape[-1]),
                table[parity],
                preferred_element_type=F32,
            )
        )
    shift = lv.wide - lv.channel
    both = total[0][:, : lv.channel] + total[1][:, shift:]
    parts = []
    for j in range(lv.slots):
        first = j * 2 * lv.targets
        part = both[first : first + lv.targets] + both[first + lv.targets : first + 2 * lv.targets]
        parts.append(part.astype(BF16))
    out[...] = jnp.concatenate(parts, axis=1)


def operator_copies(lv, operators, table, sem):
    shift = lv.wide - lv.channel
    result = []
    for op in range(lv.ops):
        first = op * lv.channel - (op % 2) * shift
        result.append(
            pltpu.make_async_copy(
                operators.at[:, pl.ds(first, lv.wide)],
                table.at[op % 2, pl.ds(op // 2 * lv.wide, lv.channel), :],
                sem.at[op],
            )
        )
    return result


def kernel(levels, nd, nb, *refs):
    (dens1, dens2, oper1, oper2, bal1, bal2, src1, tgt1, ids1, src2, tgt2, ids2, out1, out2) = refs[:14]
    scratch = refs[14:]
    per = len(scratch) // 2
    sets = (scratch[:per], scratch[per:])
    data = (
        (dens1, oper1, bal1, src1, tgt1, ids1, out1),
        (dens2, oper2, bal2, src2, tgt2, ids2, out2),
    )
    b, d = lax.axis_index("box"), lax.axis_index("dir")

    barrier = pltpu.get_barrier_semaphore()
    for step in range(1, nd):
        pl.semaphore_signal(barrier, inc=1, device_id=(b, lax.rem(d + step, nd)), device_id_type=MESH)

    @pl.when(b > 0)
    def _():
        for to in range(nd):
            pl.semaphore_signal(barrier, inc=1, device_id=(b - 1, to), device_id_type=MESH)

    @pl.when(b < nb - 1)
    def _():
        for to in range(nd):
            pl.semaphore_signal(barrier, inc=1, device_id=(b + 1, to), device_id_type=MESH)

    loads = []
    for lv, (_, oper, *_), s in zip(levels, data, sets):
        loads += operator_copies(lv, oper, s[8], s[11])
    for load in loads:
        load.start()

    for lv, (dens, _, bal, *_), s in zip(levels, data, sets):
        sort_slots(lv, nd, dens, bal, s[0], s[1])

    sides = 1 + (b > 0).astype(jnp.int32) + (b < nb - 1).astype(jnp.int32)
    pl.semaphore_wait(barrier, sides * nd - 1)

    plans = []
    for lv, s in zip(levels, sets):
        send, ext = s[1], s[2]
        sends, receives = copies(lv, nd, nb, b, d, send, ext, (s[9], s[10]))
        plans.append((sends, receives))
        for condition, make in sends:
            under(condition, lambda make=make: make().start())

    for lv, (_, _, _, src, tgt, ids, _), s in zip(levels, data, sets):
        send, ext, left, right, counts = s[1], s[2], s[4], s[5], s[6]
        ext[lv.halo + d] = send[d]
        blank = jnp.zeros(ext.shape[1:], BF16)

        @pl.when(b == 0)
        def _():
            for i in range(lv.halo):
                ext[i] = blank

        @pl.when(b == nb - 1)
        def _():
            for i in range(lv.halo):
                ext[lv.halo + nd + i] = blank

        table = s[8]
        hole = jnp.zeros((lv.wide - lv.channel, lv.wide), BF16)
        for parity in range(2):
            for k in range(lv.ops // 2):
                table[parity, k * lv.wide + lv.channel : (k + 1) * lv.wide, :] = hole
        histogram(lv, b, src, tgt, ids, left, right, counts)

    for sends, receives in plans:
        for condition, make in receives:
            under(condition, lambda make=make: make().wait_recv())
    for load in loads:
        load.wait()

    for lv, (*_, out), s in zip(levels, data, sets):
        gather_rows(lv, s[2], s[3], s[7])
        expand(lv, s[6], s[7], s[12])
        apply_operators(lv, s[12], s[8], out)

    for sends, receives in plans:
        for condition, make in sends:
            under(condition, lambda make=make: make().wait_send())


def scratch_of(lv, nd):
    flat = BF16 if lv.rows % 16 == 0 else F32
    width = lv.slots * lv.channel
    return [
        pltpu.VMEM((lv.wedges, lv.rows, lv.channel), BF16),
        pltpu.VMEM((nd, lv.rows, width), BF16),
        pltpu.VMEM((lv.chunks, lv.rows, width), BF16),
        pltpu.VMEM((lv.span, width), flat),
        pltpu.VMEM((lv.left, lv.pairs), BF16),
        pltpu.VMEM((lv.right, lv.pairs), BF16),
        pltpu.VMEM((lv.slots, 2, lv.left, lv.right), BF16),
        pltpu.VMEM((lv.slots, 2 if lv.rest else 1, lv.depth, lv.wide), BF16),
        pltpu.VMEM((2, lv.ops // 2 * lv.wide, lv.wide), BF16),
        pltpu.SemaphoreType.DMA((3 * nd,)),
        pltpu.SemaphoreType.DMA((lv.chunks,)),
        pltpu.SemaphoreType.DMA((lv.ops,)),
        pltpu.VMEM((2, lv.slots, 2 * lv.targets, lv.ops // 2 * lv.wide), BF16),
    ]


def per_device(nd, nb, *args):
    fine = Level(args[0], args[2], args[6], nd)
    coarse = Level(args[1], args[3], args[9], nd)
    levels = (fine, coarse)
    vmem = pl.BlockSpec(memory_space=pltpu.VMEM)
    smem = pl.BlockSpec(memory_space=pltpu.SMEM)
    away = pl.BlockSpec(memory_space=pl.ANY)
    return pl.pallas_call(
        functools.partial(kernel, levels, nd, nb),
        out_shape=tuple(
            jax.ShapeDtypeStruct((lv.targets, lv.slots * lv.channel), BF16) for lv in levels
        ),
        in_specs=[vmem, vmem, away, away, smem, smem] + [vmem] * 6,
        out_specs=(vmem, vmem),
        scratch_shapes=scratch_of(fine, nd) + scratch_of(coarse, nd),
        compiler_params=pltpu.CompilerParams(
            collective_id=0, has_side_effects=True, vmem_limit_bytes=56 * 1024 * 1024
        ),
        name="translate",
    )(*args)


def solution(mesh):
    boxes, dirs = P(("box", "dir"), None), P("dir", "box")
    return jax.shard_map(
        functools.partial(per_device, mesh.shape["dir"], mesh.shape["box"]),
        mesh=mesh,
        in_specs=(boxes, boxes, P(), P(), P(), P()) + (dirs,) * 6,
        out_specs=(P("box", "dir"), P("box", "dir")),
        check_vma=False,
    )
```

profile of v0, /device:TPU:1, one launch (start us, length us, event | category | flops | bytes accessed | tf_op | source)
XLA Modules:
  0.0 22.2 jit_solution(10803654174267001344)
XLA Ops:
  0.6 18.5 %translate.1 = (bf16[128,384]{1,0:T(8,128)(2,1)}, bf16[64,768]{1,0:T(8,128)(2,1)}) custom-call(bf16[32,1536]{1,0:T(8,128)(2,1)} %refs_0_.1, bf16[16,3072]{1,0:T(8,128)(2,1)} %refs_1_.1, bf16[192,3072]{1,0:T(8,128)(2,1)} %refs_2_.1, bf16[192,3072]{1,0:T(8,128)(2,1)} %refs_3_.1, s32[8]{0:T(128)} %refs_4_.1, s32[16]{0:T(128)} %refs_5_.1, s32[2,2048]{1,0:T(2,128)} %refs_6_.1, ...), custom_call_target="tpu_custom_call" | custom-call | tf_op jit(solution)/shard_map/translate/pallas_call | solution.py:308
  19.2 1.5 %copy.16 = bf16[128,384]{1,0:T(8,128)(2,1)} copy(bf16[128,384]{1,0:T(8,128)(2,1)} %get-tuple-element.4) | data formatting | bytes 196608
  20.7 1.5 %copy.17 = bf16[64,768]{1,0:T(8,128)(2,1)} copy(bf16[64,768]{1,0:T(8,128)(2,1)} %get-tuple-element.5) | data formatting | bytes 196608
where the time goes:
time: 22.5 us; the launch traced here: 22.2 us
  Pallas kernels  18.5 us (82%)
  local copies, waits for them, and re-layouts  3.08 us (14%)
  between operations  0.64 us (3%)
    pallas_call x1, Pallas kernels, per_device(): pl.pallas_call(functools.partial(kernel, levels, nd, nb), out_shape=tuple...  18.5 us
    unnamed x2, local copies, waits for them, and re-layouts  3.08 us

commit v1 on v0

--- a/solution.py
+++ b/solution.py
@@ -36,10 +36,12 @@
         self.wide = -(-self.channel // LANES) * LANES
 
 
-def one_hot(out, at, key, count):
+def one_hot(out, key, count):
     row = lax.broadcasted_iota(jnp.int32, (LANES, key.shape[1]), 0).astype(F32).astype(BF16)
+    block = (key // LANES).astype(F32).astype(BF16)
+    within = (key % LANES).astype(F32).astype(BF16)
     for base in range(0, count, LANES):
-        near = (key - base).astype(F32).astype(BF16)
+        near = jnp.where(block == jnp.asarray(base // LANES, BF16), within, -jnp.ones((), BF16))
         hot = jnp.where(near == row, jnp.ones((), BF16), jnp.zeros((), BF16))
         out[base : base + LANES, :] = hot
 
@@ -101,8 +103,8 @@
         if lv.rest:
             tail = lv.lo * lv.full + low * lv.rest + (source - lv.full)
             key = jnp.where(source < lv.full, key, tail)
-        one_hot(left, None, high * lv.targets + target, lv.left)
-        one_hot(right, None, key, lv.right)
+        one_hot(left, high * lv.targets + target, lv.left)
+        one_hot(right, key, lv.right)
         found = lax.dot_general(
             left[...], right[...], (((1,), (1,)), ((), ())), preferred_element_type=F32
         )
@@ -206,6 +208,14 @@
     )
     b, d = lax.axis_index("box"), lax.axis_index("dir")
 
+    firsts = []
+    for (dens, _, _, src, tgt, ids, _), s in zip(data, sets):
+        moves = zip((dens, src, tgt, ids), s[14:18])
+        firsts.append([pltpu.make_async_copy(a, v, s[13].at[i]) for i, (a, v) in enumerate(moves)])
+    for i in range(4):
+        for first in firsts:
+            first[i].start()
+
     barrier = pltpu.get_barrier_semaphore()
     for step in range(1, nd):
         pl.semaphore_signal(barrier, inc=1, device_id=(b, lax.rem(d + step, nd)), device_id_type=MESH)
@@ -226,8 +236,9 @@
     for load in loads:
         load.start()
 
-    for lv, (dens, _, bal, *_), s in zip(levels, data, sets):
-        sort_slots(lv, nd, dens, bal, s[0], s[1])
+    for lv, (_, _, bal, *_), s, first in zip(levels, data, sets, firsts):
+        first[0].wait()
+        sort_slots(lv, nd, s[14], bal, s[0], s[1])
 
     sides = 1 + (b > 0).astype(jnp.int32) + (b < nb - 1).astype(jnp.int32)
     pl.semaphore_wait(barrier, sides * nd - 1)
@@ -240,8 +251,11 @@
         for condition, make in sends:
             under(condition, lambda make=make: make().start())
 
-    for lv, (_, _, _, src, tgt, ids, _), s in zip(levels, data, sets):
+    for lv, s, waits in zip(levels, sets, firsts):
+        src, tgt, ids = s[15:18]
         send, ext, left, right, counts = s[1], s[2], s[4], s[5], s[6]
+        for wait in waits[1:]:
+            wait.wait()
         ext[lv.halo + d] = send[d]
         blank = jnp.zeros(ext.shape[1:], BF16)
 
@@ -268,14 +282,30 @@
     for load in loads:
         load.wait()
 
+    results = []
     for lv, (*_, out), s in zip(levels, data, sets):
         gather_rows(lv, s[2], s[3], s[7])
         expand(lv, s[6], s[7], s[12])
-        apply_operators(lv, s[12], s[8], out)
+        apply_operators(lv, s[12], s[8], s[18])
+        results.append(pltpu.make_async_copy(s[18], out, s[13].at[4]))
+        results[-1].start()
 
     for sends, receives in plans:
         for condition, make in sends:
             under(condition, lambda make=make: make().wait_send())
+    for result in results:
+        result.wait()
+
+
+def hand_on(one, two, out1, out2, sem):
+    moves = [
+        pltpu.make_async_copy(one, out1, sem.at[0]),
+        pltpu.make_async_copy(two, out2, sem.at[1]),
+    ]
+    for move in moves:
+        move.start()
+    for move in moves:
+        move.wait()
 
 
 def scratch_of(lv, nd):
@@ -295,6 +325,12 @@
         pltpu.SemaphoreType.DMA((lv.chunks,)),
         pltpu.SemaphoreType.DMA((lv.ops,)),
         pltpu.VMEM((2, lv.slots, 2 * lv.targets, lv.ops // 2 * lv.wide), BF16),
+        pltpu.SemaphoreType.DMA((5,)),
+        pltpu.VMEM((lv.rows, lv.wedges * lv.channel), BF16),
+        pltpu.VMEM((lv.slots, lv.pairs), jnp.int32),
+        pltpu.VMEM((lv.slots, lv.pairs), jnp.int32),
+        pltpu.VMEM((lv.slots, lv.pairs), jnp.int32),
+        pltpu.VMEM((lv.targets, width), BF16),
     ]
 
 
@@ -302,22 +338,31 @@
     fine = Level(args[0], args[2], args[6], nd)
     coarse = Level(args[1], args[3], args[9], nd)
     levels = (fine, coarse)
-    vmem = pl.BlockSpec(memory_space=pltpu.VMEM)
     smem = pl.BlockSpec(memory_space=pltpu.SMEM)
     away = pl.BlockSpec(memory_space=pl.ANY)
-    return pl.pallas_call(
+    shapes = tuple(
+        jax.ShapeDtypeStruct((lv.targets, lv.slots * lv.channel), BF16) for lv in levels
+    )
+    found = pl.pallas_call(
         functools.partial(kernel, levels, nd, nb),
-        out_shape=tuple(
-            jax.ShapeDtypeStruct((lv.targets, lv.slots * lv.channel), BF16) for lv in levels
-        ),
-        in_specs=[vmem, vmem, away, away, smem, smem] + [vmem] * 6,
-        out_specs=(vmem, vmem),
+        out_shape=shapes,
+        in_specs=[away] * 4 + [smem] * 2 + [away] * 6,
+        out_specs=(away, away),
         scratch_shapes=scratch_of(fine, nd) + scratch_of(coarse, nd),
         compiler_params=pltpu.CompilerParams(
             collective_id=0, has_side_effects=True, vmem_limit_bytes=56 * 1024 * 1024
         ),
         name="translate",
     )(*args)
+    return pl.pallas_call(
+        hand_on,
+        out_shape=shapes,
+        in_specs=[away] * 2,
+        out_specs=(away, away),
+        scratch_shapes=[pltpu.SemaphoreType.DMA((2,))],
+        compiler_params=pltpu.CompilerParams(vmem_limit_bytes=60 * 1024 * 1024),
+        name="hand_on",
+    )(*found)
 
 
 def solution(mesh):

time: 22.5 us -> 26.2 us (1.16)
  Pallas kernels: 18.5 us -> 25.4 us
  local copies, waits for them, and re-layouts: 3.08 us -> 0 us
    pallas_call x1 -> x2, Pallas kernels: 18.5 us -> 25.4 us  [the longest x1 18.3 us: per_device(): pl.pallas_call(functools.partial(kernel, levels, nd, nb), out_shape=shape...]
    unnamed x2 -> x0, local copies, waits for them, and re-layouts: 3.08 us -> none
where the time goes in v1:
time: 26.2 us; the launch traced here: 26 us
  Pallas kernels  25.4 us (97%)
  between operations  0.64 us (2%)
    pallas_call x1, Pallas kernels, per_device(): pl.pallas_call(functools.partial(kernel, levels, nd, nb), out_shape=shape...  18.3 us
    pallas_call x1, Pallas kernels, per_device(): pl.pallas_call(hand_on, out_shape=shapes, in_specs=[away] * 2, out_specs=...  7.08 us

profile of v1, /device:TPU:1, one launch (start us, length us, event | category | flops | bytes accessed | tf_op | source)
XLA Modules:
  0.0 26.0 jit_solution(16771253180915596506)
XLA Ops:
  0.6 18.3 %translate.1 = (bf16[128,384]{1,0:T(8,128)(2,1)}, bf16[64,768]{1,0:T(8,128)(2,1)}) custom-call(bf16[32,1536]{1,0:T(8,128)(2,1)} %refs_0_.1, bf16[16,3072]{1,0:T(8,128)(2,1)} %refs_1_.1, bf16[192,3072]{1,0:T(8,128)(2,1)} %refs_2_.1, bf16[192,3072]{1,0:T(8,128)(2,1)} %refs_3_.1, s32[8]{0:T(128)} %refs_4_.1, s32[16]{0:T(128)} %refs_5_.1, s32[2,2048]{1,0:T(2,128)} %refs_6_.1, ...), custom_call_target="tpu_custom_call" | custom-call | tf_op jit(solution)/shard_map/translate/pallas_call | solution.py:346
  18.9 7.1 %hand_on.1 = (bf16[128,384]{1,0:T(8,128)(2,1)}, bf16[64,768]{1,0:T(8,128)(2,1)}) custom-call(bf16[128,384]{1,0:T(8,128)(2,1)} %get-tuple-element.4.one, bf16[64,768]{1,0:T(8,128)(2,1)} %get-tuple-element.5.two), custom_call_target="tpu_custom_call" | custom-call | tf_op jit(solution)/shard_map/hand_on/pallas_call | solution.py:357

commit v2 on v1

--- a/solution.py
+++ b/solution.py
@@ -11,6 +11,7 @@
 LANES = 128
 BF16 = jnp.bfloat16
 F32 = jnp.float32
+HOT = jnp.float8_e4m3fn
 MESH = pl.DeviceIdType.MESH
 
 
@@ -43,7 +44,7 @@
     for base in range(0, count, LANES):
         near = jnp.where(block == jnp.asarray(base // LANES, BF16), within, -jnp.ones((), BF16))
         hot = jnp.where(near == row, jnp.ones((), BF16), jnp.zeros((), BF16))
-        out[base : base + LANES, :] = hot
+        out[base : base + LANES, :] = hot.astype(out.dtype)
 
 
 def sort_slots(lv, nd, density, balance, split, send):
@@ -297,15 +298,9 @@
         result.wait()
 
 
-def hand_on(one, two, out1, out2, sem):
-    moves = [
-        pltpu.make_async_copy(one, out1, sem.at[0]),
-        pltpu.make_async_copy(two, out2, sem.at[1]),
-    ]
-    for move in moves:
-        move.start()
-    for move in moves:
-        move.wait()
+def hand_on(one, two, out1, out2):
+    out1[...] = one[...]
+    out2[...] = two[...]
 
 
 def scratch_of(lv, nd):
@@ -316,8 +311,8 @@
         pltpu.VMEM((nd, lv.rows, width), BF16),
         pltpu.VMEM((lv.chunks, lv.rows, width), BF16),
         pltpu.VMEM((lv.span, width), flat),
-        pltpu.VMEM((lv.left, lv.pairs), BF16),
-        pltpu.VMEM((lv.right, lv.pairs), BF16),
+        pltpu.VMEM((lv.left, lv.pairs), HOT),
+        pltpu.VMEM((lv.right, lv.pairs), HOT),
         pltpu.VMEM((lv.slots, 2, lv.left, lv.right), BF16),
         pltpu.VMEM((lv.slots, 2 if lv.rest else 1, lv.depth, lv.wide), BF16),
         pltpu.VMEM((2, lv.ops // 2 * lv.wide, lv.wide), BF16),
@@ -357,9 +352,6 @@
     return pl.pallas_call(
         hand_on,
         out_shape=shapes,
-        in_specs=[away] * 2,
-        out_specs=(away, away),
-        scratch_shapes=[pltpu.SemaphoreType.DMA((2,))],
         compiler_params=pltpu.CompilerParams(vmem_limit_bytes=60 * 1024 * 1024),
         name="hand_on",
     )(*found)

time: 26.2 us -> 19.4 us (0.74)
  the two profiles are of different devices: /device:TPU:1 before, /device:TPU:0 now
where the time goes in v2:
time: 19.4 us; the launch traced here: 19.3 us
  Pallas kernels  18.6 us (96%)
  between operations  0.64 us (3%)
    pallas_call x1, Pallas kernels, per_device(): pl.pallas_call(functools.partial(kernel, levels, nd, nb), out_shape=shape...  17 us
    pallas_call x1, Pallas kernels, per_device(): pl.pallas_call(hand_on, out_shape=shapes, compiler_params=pltpu.CompilerP...  1.62 us

profile of v2, /device:TPU:0, one launch (start us, length us, event | category | flops | bytes accessed | tf_op | source)
XLA Modules:
  0.0 19.3 jit_solution(17927549017583319241)
XLA Ops:
  0.6 17.0 %translate.1 = (bf16[128,384]{1,0:T(8,128)(2,1)}, bf16[64,768]{1,0:T(8,128)(2,1)}) custom-call(bf16[32,1536]{1,0:T(8,128)(2,1)} %refs_0_.1, bf16[16,3072]{1,0:T(8,128)(2,1)} %refs_1_.1, bf16[192,3072]{1,0:T(8,128)(2,1)} %refs_2_.1, bf16[192,3072]{1,0:T(8,128)(2,1)} %refs_3_.1, s32[8]{0:T(128)} %refs_4_.1, s32[16]{0:T(128)} %refs_5_.1, s32[2,2048]{1,0:T(2,128)} %refs_6_.1, ...), custom_call_target="tpu_custom_call" | custom-call | tf_op jit(solution)/shard_map/translate/pallas_call | solution.py:341
  17.7 1.6 %hand_on.1 = (bf16[128,384]{1,0:T(8,128)(2,1)}, bf16[64,768]{1,0:T(8,128)(2,1)}) custom-call(bf16[128,384]{1,0:T(8,128)(2,1)} %get-tuple-element.4.one, bf16[64,768]{1,0:T(8,128)(2,1)} %get-tuple-element.5.two), custom_call_target="tpu_custom_call" | custom-call | tf_op jit(solution)/shard_map/hand_on/pallas_call | solution.py:352

commit v3 on v2

--- a/solution.py
+++ b/solution.py
@@ -37,14 +37,18 @@
         self.wide = -(-self.channel // LANES) * LANES
 
 
-def one_hot(out, key, count):
-    row = lax.broadcasted_iota(jnp.int32, (LANES, key.shape[1]), 0).astype(F32).astype(BF16)
-    block = (key // LANES).astype(F32).astype(BF16)
-    within = (key % LANES).astype(F32).astype(BF16)
-    for base in range(0, count, LANES):
-        near = jnp.where(block == jnp.asarray(base // LANES, BF16), within, -jnp.ones((), BF16))
+def one_hot_pieces(out, key, count):
+    row = lax.broadcasted_iota(jnp.int32, (LANES, LANES), 0).astype(F32).astype(BF16)
+    row = jnp.concatenate([row] * (key.shape[1] // LANES), axis=1)
+    block = lax.shift_right_logical(key, LANES.bit_length() - 1).astype(F32).astype(BF16)
+    within = jnp.bitwise_and(key, LANES - 1).astype(F32).astype(BF16)
+
+    def piece(k):
+        near = jnp.where(block == jnp.asarray(k, BF16), within, -jnp.ones((), BF16))
         hot = jnp.where(near == row, jnp.ones((), BF16), jnp.zeros((), BF16))
-        out[base : base + LANES, :] = hot.astype(out.dtype)
+        out[k * LANES : (k + 1) * LANES, :] = hot.astype(out.dtype)
+
+    return [functools.partial(piece, k) for k in range(count // LANES)]
 
 
 def sort_slots(lv, nd, density, balance, split, send):
@@ -93,28 +97,45 @@
         pl.when(condition)(act)
 
 
-def histogram(lv, b, sources, targets, op_ids, left, right, counts):
-    def body(j, _):
-        at = pl.ds(j, 1)
-        op = op_ids[at, :]
-        high, low = op // lv.lo, op % lv.lo
-        source = sources[at, :] - (b * lv.targets - RIM)
-        target = targets[at, :] - b * lv.targets
-        key = low * lv.full + source
-        if lv.rest:
-            tail = lv.lo * lv.full + low * lv.rest + (source - lv.full)
-            key = jnp.where(source < lv.full, key, tail)
-        one_hot(left, high * lv.targets + target, lv.left)
-        one_hot(right, key, lv.right)
+def hot_pieces(lv, b, j, sources, targets, op_ids, left, right):
+    at = slice(j, j + 1)
+    op = op_ids[at, :]
+    high = lax.shift_right_logical(op, lv.lo.bit_length() - 1)
+    low = jnp.bitwise_and(op, lv.lo - 1)
+    source = sources[at, :] - (b * lv.targets - RIM)
+    target = targets[at, :] - b * lv.targets
+    key = low * lv.full + source
+    if lv.rest:
+        tail = lv.lo * lv.full + low * lv.rest + (source - lv.full)
+        key = jnp.where(source < lv.full, key, tail)
+    return one_hot_pieces(left, high * lv.targets + target, lv.left) + one_hot_pieces(
+        right, key, lv.right
+    )
+
+
+def count_pieces(lv, j, left, right, counts):
+    def piece(columns):
         found = lax.dot_general(
-            left[...], right[...], (((1,), (1,)), ((), ())), preferred_element_type=F32
+            left[...], right[columns, :], (((1,), (1,)), ((), ())), preferred_element_type=F32
         )
         main = found.astype(BF16)
-        counts[j, 0] = main
-        counts[j, 1] = (found - main.astype(F32)).astype(BF16)
-        return 0
-
-    lax.fori_loop(0, lv.slots, body, 0)
+        counts[j, 0, :, columns] = main
+        counts[j, 1, :, columns] = (found - main.astype(F32)).astype(BF16)
+
+    step = 2 * LANES
+    return [functools.partial(piece, slice(c, c + step)) for c in range(0, lv.right, step)]
+
+
+def interleave(first, second):
+    done = 0
+    for i, act in enumerate(second):
+        until = (i + 1) * len(first) // len(second)
+        for other in first[done:until]:
+            other()
+        done = until
+        act()
+    for other in first[done:]:
+        other()
 
 
 def gather_rows(lv, ext, flat, weights):
@@ -133,7 +154,7 @@
 
 
 def expand(lv, counts, weights, grown):
-    def body(j, _):
+    def body(j):
         for low in range(lv.lo):
             picked = []
             for term in range(2):
@@ -157,9 +178,9 @@
                 rows = slice(high * lv.targets, (high + 1) * lv.targets)
                 grown[op % 2, j, : lv.targets, column : column + lv.wide] = main[rows]
                 grown[op % 2, j, lv.targets :, column : column + lv.wide] = rest[rows]
-        return 0
-
-    lax.fori_loop(0, lv.slots, body, 0)
+
+    for j in range(lv.slots):
+        body(j)
 
 
 def apply_operators(lv, grown, table, out):
@@ -231,11 +252,11 @@
         for to in range(nd):
             pl.semaphore_signal(barrier, inc=1, device_id=(b + 1, to), device_id_type=MESH)
 
-    loads = []
+    tables = []
     for lv, (_, oper, *_), s in zip(levels, data, sets):
-        loads += operator_copies(lv, oper, s[8], s[11])
-    for load in loads:
-        load.start()
+        tables.append(operator_copies(lv, oper, s[8], s[11]))
+        for load in tables[-1]:
+            load.start()
 
     for lv, (_, _, bal, *_), s, first in zip(levels, data, sets, firsts):
         first[0].wait()
@@ -252,9 +273,10 @@
         for condition, make in sends:
             under(condition, lambda make=make: make().start())
 
+    jobs = []
     for lv, s, waits in zip(levels, sets, firsts):
         src, tgt, ids = s[15:18]
-        send, ext, left, right, counts = s[1], s[2], s[4], s[5], s[6]
+        send, ext, lefts, rights, counts = s[1], s[2], s[4], s[5], s[6]
         for wait in waits[1:]:
             wait.wait()
         ext[lv.halo + d] = send[d]
@@ -275,16 +297,26 @@
         for parity in range(2):
             for k in range(lv.ops // 2):
                 table[parity, k * lv.wide + lv.channel : (k + 1) * lv.wide, :] = hole
-        histogram(lv, b, src, tgt, ids, left, right, counts)
-
-    for sends, receives in plans:
+        for j in range(lv.slots):
+            left, right = lefts.at[j % 2], rights.at[j % 2]
+            jobs.append(
+                (
+                    functools.partial(hot_pieces, lv, b, j, src, tgt, ids, left, right),
+                    functools.partial(count_pieces, lv, j, left, right, counts),
+                )
+            )
+
+    for act in jobs[0][0]():
+        act()
+    for i, (_, count) in enumerate(jobs):
+        interleave(jobs[i + 1][0]() if i + 1 < len(jobs) else [], count())
+
+    results = []
+    for lv, (*_, out), s, (_, receives), loads in zip(levels, data, sets, plans, tables):
         for condition, make in receives:
             under(condition, lambda make=make: make().wait_recv())
-    for load in loads:
-        load.wait()
-
-    results = []
-    for lv, (*_, out), s in zip(levels, data, sets):
+        for load in loads:
+            load.wait()
         gather_rows(lv, s[2], s[3], s[7])
         expand(lv, s[6], s[7], s[12])
         apply_operators(lv, s[12], s[8], s[18])
@@ -311,8 +343,8 @@
         pltpu.VMEM((nd, lv.rows, width), BF16),
         pltpu.VMEM((lv.chunks, lv.rows, width), BF16),
         pltpu.VMEM((lv.span, width), flat),
-        pltpu.VMEM((lv.left, lv.pairs), HOT),
-        pltpu.VMEM((lv.right, lv.pairs), HOT),
+        pltpu.VMEM((2, lv.left, lv.pairs), HOT),
+        pltpu.VMEM((2, lv.right, lv.pairs), HOT),
         pltpu.VMEM((lv.slots, 2, lv.left, lv.right), BF16),
         pltpu.VMEM((lv.slots, 2 if lv.rest else 1, lv.depth, lv.wide), BF16),
         pltpu.VMEM((2, lv.ops // 2 * lv.wide, lv.wide), BF16),

time: 19.4 us -> 16.7 us (0.86)
  the two profiles are of different devices: /device:TPU:0 before, /device:TPU:1 now
where the time goes in v3:
time: 16.7 us; the launch traced here: 16.5 us
  Pallas kernels  15.8 us (95%)
  between operations  0.64 us (4%)
    pallas_call x1, Pallas kernels, per_device(): pl.pallas_call(functools.partial(kernel, levels, nd, nb), out_shape=shape...  14.2 us
    pallas_call x1, Pallas kernels, per_device(): pl.pallas_call(hand_on, out_shape=shapes, compiler_params=pltpu.CompilerP...  1.62 us

profile of v3, /device:TPU:1, one launch (start us, length us, event | category | flops | bytes accessed | tf_op | source)
XLA Modules:
  0.0 16.5 jit_solution(12394477723096985907)
XLA Ops:
  0.6 14.2 %translate.1 = (bf16[128,384]{1,0:T(8,128)(2,1)}, bf16[64,768]{1,0:T(8,128)(2,1)}) custom-call(bf16[32,1536]{1,0:T(8,128)(2,1)} %refs_0_.1, bf16[16,3072]{1,0:T(8,128)(2,1)} %refs_1_.1, bf16[192,3072]{1,0:T(8,128)(2,1)} %refs_2_.1, bf16[192,3072]{1,0:T(8,128)(2,1)} %refs_3_.1, s32[8]{0:T(128)} %refs_4_.1, s32[16]{0:T(128)} %refs_5_.1, s32[2,2048]{1,0:T(2,128)} %refs_6_.1, ...), custom_call_target="tpu_custom_call" | custom-call | tf_op jit(solution)/shard_map/translate/pallas_call | solution.py:373
  14.9 1.6 %hand_on.1 = (bf16[128,384]{1,0:T(8,128)(2,1)}, bf16[64,768]{1,0:T(8,128)(2,1)}) custom-call(bf16[128,384]{1,0:T(8,128)(2,1)} %get-tuple-element.4.one, bf16[64,768]{1,0:T(8,128)(2,1)} %get-tuple-element.5.two), custom_call_target="tpu_custom_call" | custom-call | tf_op jit(solution)/shard_map/hand_on/pallas_call | solution.py:384

commit v4 on v3

--- a/solution.py
+++ b/solution.py
@@ -59,42 +59,41 @@
         send[d] = jnp.concatenate(parts, axis=1)
 
 
-def copies(lv, nd, nb, b, d, send, ext, sems):
-    send_sem, recv_sem = sems
-
-    def copy(to_box, to_dir, chunk, sem):
-        return pltpu.make_async_remote_copy(
-            src_ref=send.at[to_dir],
-            dst_ref=ext.at[chunk],
-            send_sem=send_sem.at[sem],
-            recv_sem=recv_sem.at[chunk],
-            device_id=(to_box, to_dir),
-            device_id_type=MESH,
+def exchange(lv, nd, b, d, send, ext, send_sem, recv_sem):
+    result = []
+    for step in range(1, nd):
+        to = lax.rem(d + step, nd)
+        result.append(
+            pltpu.make_async_remote_copy(
+                src_ref=send.at[to],
+                dst_ref=ext.at[lv.halo + d],
+                send_sem=send_sem.at[step],
+                recv_sem=recv_sem.at[nd - step],
+                device_id=(b, to),
+                device_id_type=MESH,
+            )
         )
-
-    sends, receives = [], []
-    for step in range(nd):
-        to = lax.rem(d + step, nd)
-        up = jnp.logical_and(d >= nd - lv.halo, b < nb - 1)
-        down = jnp.logical_and(d < lv.halo, b > 0)
-        if step:
-            sends.append((None, functools.partial(copy, b, to, lv.halo + d, step)))
-        sends.append((up, functools.partial(copy, b + 1, to, d - (nd - lv.halo), nd + step)))
-        sends.append((down, functools.partial(copy, b - 1, to, lv.halo + nd + d, 2 * nd + step)))
-    for step in range(1, nd):
-        chunk = lv.halo + lax.rem(d + step, nd)
-        receives.append((None, functools.partial(copy, b, d, chunk, 0)))
-    for i in range(lv.halo):
-        receives.append((b > 0, functools.partial(copy, b, d, i, 0)))
-        receives.append((b < nb - 1, functools.partial(copy, b, d, lv.halo + nd + i, 0)))
-    return sends, receives
-
-
-def under(condition, act):
-    if condition is None:
-        act()
-    else:
-        pl.when(condition)(act)
+    return result
+
+
+def halo_copies(lv, nd, nb, b, d, ext, sem):
+    up = pltpu.make_async_remote_copy(
+        src_ref=ext.at[pl.ds(nd, lv.halo)],
+        dst_ref=ext.at[pl.ds(0, lv.halo)],
+        send_sem=sem.at[0],
+        recv_sem=sem.at[1],
+        device_id=(b + 1, d),
+        device_id_type=MESH,
+    )
+    down = pltpu.make_async_remote_copy(
+        src_ref=ext.at[pl.ds(lv.halo, lv.halo)],
+        dst_ref=ext.at[pl.ds(lv.halo + nd, lv.halo)],
+        send_sem=sem.at[2],
+        recv_sem=sem.at[3],
+        device_id=(b - 1, d),
+        device_id_type=MESH,
+    )
+    return [(b < nb - 1, b > 0, up), (b > 0, b < nb - 1, down)]
 
 
 def hot_pieces(lv, b, j, sources, targets, op_ids, left, right):
@@ -228,6 +227,7 @@
         (dens1, oper1, bal1, src1, tgt1, ids1, out1),
         (dens2, oper2, bal2, src2, tgt2, ids2, out2),
     )
+    fine_slots, coarse_slots = (lv.slots for lv in levels)
     b, d = lax.axis_index("box"), lax.axis_index("dir")
 
     firsts = []
@@ -244,13 +244,11 @@
 
     @pl.when(b > 0)
     def _():
-        for to in range(nd):
-            pl.semaphore_signal(barrier, inc=1, device_id=(b - 1, to), device_id_type=MESH)
+        pl.semaphore_signal(barrier, inc=1, device_id=(b - 1, d), device_id_type=MESH)
 
     @pl.when(b < nb - 1)
     def _():
-        for to in range(nd):
-            pl.semaphore_signal(barrier, inc=1, device_id=(b + 1, to), device_id_type=MESH)
+        pl.semaphore_signal(barrier, inc=1, device_id=(b + 1, d), device_id_type=MESH)
 
     tables = []
     for lv, (_, oper, *_), s in zip(levels, data, sets):
@@ -262,41 +260,12 @@
         first[0].wait()
         sort_slots(lv, nd, s[14], bal, s[0], s[1])
 
-    sides = 1 + (b > 0).astype(jnp.int32) + (b < nb - 1).astype(jnp.int32)
-    pl.semaphore_wait(barrier, sides * nd - 1)
-
-    plans = []
-    for lv, s in zip(levels, sets):
-        send, ext = s[1], s[2]
-        sends, receives = copies(lv, nd, nb, b, d, send, ext, (s[9], s[10]))
-        plans.append((sends, receives))
-        for condition, make in sends:
-            under(condition, lambda make=make: make().start())
-
     jobs = []
     for lv, s, waits in zip(levels, sets, firsts):
         src, tgt, ids = s[15:18]
-        send, ext, lefts, rights, counts = s[1], s[2], s[4], s[5], s[6]
+        lefts, rights, counts = s[4], s[5], s[6]
         for wait in waits[1:]:
             wait.wait()
-        ext[lv.halo + d] = send[d]
-        blank = jnp.zeros(ext.shape[1:], BF16)
-
-        @pl.when(b == 0)
-        def _():
-            for i in range(lv.halo):
-                ext[i] = blank
-
-        @pl.when(b == nb - 1)
-        def _():
-            for i in range(lv.halo):
-                ext[lv.halo + nd + i] = blank
-
-        table = s[8]
-        hole = jnp.zeros((lv.wide - lv.channel, lv.wide), BF16)
-        for parity in range(2):
-            for k in range(lv.ops // 2):
-                table[parity, k * lv.wide + lv.channel : (k + 1) * lv.wide, :] = hole
         for j in range(lv.slots):
             left, right = lefts.at[j % 2], rights.at[j % 2]
             jobs.append(
@@ -305,16 +274,53 @@
                     functools.partial(count_pieces, lv, j, left, right, counts),
                 )
             )
-
     for act in jobs[0][0]():
         act()
+
+    sides = (b > 0).astype(jnp.int32) + (b < nb - 1).astype(jnp.int32)
+    pl.semaphore_wait(barrier, nd - 1 + sides)
+    swaps, halos = [], []
+    for lv, s in zip(levels, sets):
+        swaps.append(exchange(lv, nd, b, d, s[1], s[2], s[9], s[10]))
+        for swap in swaps[-1]:
+            swap.start()
+    for lv, s in zip(levels, sets):
+        halos.append(halo_copies(lv, nd, nb, b, d, s[2], s[19]))
+        send, ext, table = s[1], s[2], s[8]
+        ext[lv.halo + d] = send[d]
+        blank = jnp.zeros(ext.shape[1:], BF16)
+
+        @pl.when(b == 0)
+        def _():
+            for i in range(lv.halo):
+                ext[i] = blank
+
+        @pl.when(b == nb - 1)
+        def _():
+            for i in range(lv.halo):
+                ext[lv.halo + nd + i] = blank
+
+        hole = jnp.zeros((lv.wide - lv.channel, lv.wide), BF16)
+        for parity in range(2):
+            for k in range(lv.ops // 2):
+                table[parity, k * lv.wide + lv.channel : (k + 1) * lv.wide, :] = hole
+
+    def hand_halos(level):
+        for swap in swaps[level]:
+            swap.wait_recv()
+        for sends, _, copy in halos[level]:
+            pl.when(sends)(copy.start)
+
+    after = {fine_slots - 1: 0, fine_slots + coarse_slots // 2 - 1: 1}
     for i, (_, count) in enumerate(jobs):
         interleave(jobs[i + 1][0]() if i + 1 < len(jobs) else [], count())
+        if i in after:
+            hand_halos(after[i])
 
     results = []
-    for lv, (*_, out), s, (_, receives), loads in zip(levels, data, sets, plans, tables):
-        for condition, make in receives:
-            under(condition, lambda make=make: make().wait_recv())
+    for lv, (*_, out), s, halo, loads in zip(levels, data, sets, halos, tables):
+        for _, receives, copy in halo:
+            pl.when(receives)(copy.wait_recv)
         for load in loads:
             load.wait()
         gather_rows(lv, s[2], s[3], s[7])
@@ -323,9 +329,11 @@
         results.append(pltpu.make_async_copy(s[18], out, s[13].at[4]))
         results[-1].start()
 
-    for sends, receives in plans:
-        for condition, make in sends:
-            under(condition, lambda make=make: make().wait_send())
+    for swap, halo in zip(swaps, halos):
+        for copy in swap:
+            copy.wait_send()
+        for sends, _, copy in halo:
+            pl.when(sends)(copy.wait_send)
     for result in results:
         result.wait()
 
@@ -348,8 +356,8 @@
         pltpu.VMEM((lv.slots, 2, lv.left, lv.right), BF16),
         pltpu.VMEM((lv.slots, 2 if lv.rest else 1, lv.depth, lv.wide), BF16),
         pltpu.VMEM((2, lv.ops // 2 * lv.wide, lv.wide), BF16),
-        pltpu.SemaphoreType.DMA((3 * nd,)),
-        pltpu.SemaphoreType.DMA((lv.chunks,)),
+        pltpu.SemaphoreType.DMA((nd,)),
+        pltpu.SemaphoreType.DMA((nd,)),
         pltpu.SemaphoreType.DMA((lv.ops,)),
         pltpu.VMEM((2, lv.slots, 2 * lv.targets, lv.ops // 2 * lv.wide), BF16),
         pltpu.SemaphoreType.DMA((5,)),
@@ -358,6 +366,7 @@
         pltpu.VMEM((lv.slots, lv.pairs), jnp.int32),
         pltpu.VMEM((lv.slots, lv.pairs), jnp.int32),
         pltpu.VMEM((lv.targets, width), BF16),
+        pltpu.SemaphoreType.DMA((4,)),
     ]
 
 

time: 16.7 us -> 19.3 us (1.16)
  Pallas kernels: 15.8 us -> 18.5 us
    pallas_call x1, Pallas kernels: 14.2 us -> 16.9 us  [per_device(): pl.pallas_call(functools.partial(kernel, levels, nd, nb), out_shape=shape...]
where the time goes in v4:
time: 19.3 us; the launch traced here: 19.1 us
  Pallas kernels  18.5 us (96%)
  between operations  0.64 us (3%)
    pallas_call x1, Pallas kernels, per_device(): pl.pallas_call(functools.partial(kernel, levels, nd, nb), out_shape=shape...  16.9 us
    pallas_call x1, Pallas kernels, per_device(): pl.pallas_call(hand_on, out_shape=shapes, compiler_params=pltpu.CompilerP...  1.62 us

profile of v4, /device:TPU:1, one launch (start us, length us, event | category | flops | bytes accessed | tf_op | source)
XLA Modules:
  0.0 19.1 jit_solution(17818828685713289547)
XLA Ops:
  0.6 16.9 %translate.1 = (bf16[128,384]{1,0:T(8,128)(2,1)}, bf16[64,768]{1,0:T(8,128)(2,1)}) custom-call(bf16[32,1536]{1,0:T(8,128)(2,1)} %refs_0_.1, bf16[16,3072]{1,0:T(8,128)(2,1)} %refs_1_.1, bf16[192,3072]{1,0:T(8,128)(2,1)} %refs_2_.1, bf16[192,3072]{1,0:T(8,128)(2,1)} %refs_3_.1, s32[8]{0:T(128)} %refs_4_.1, s32[16]{0:T(128)} %refs_5_.1, s32[2,2048]{1,0:T(2,128)} %refs_6_.1, ...), custom_call_target="tpu_custom_call" | custom-call | tf_op jit(solution)/shard_map/translate/pallas_call | solution.py:382
  17.5 1.6 %hand_on.1 = (bf16[128,384]{1,0:T(8,128)(2,1)}, bf16[64,768]{1,0:T(8,128)(2,1)}) custom-call(bf16[128,384]{1,0:T(8,128)(2,1)} %get-tuple-element.4.one, bf16[64,768]{1,0:T(8,128)(2,1)} %get-tuple-element.5.two), custom_call_target="tpu_custom_call" | custom-call | tf_op jit(solution)/shard_map/hand_on/pallas_call | solution.py:393

commit v5 on v3

--- a/solution.py
+++ b/solution.py
@@ -59,7 +59,7 @@
         send[d] = jnp.concatenate(parts, axis=1)
 
 
-def copies(lv, nd, nb, b, d, send, ext, sems):
+def direct_copies(lv, nd, nb, b, d, send, ext, sems):
     send_sem, recv_sem = sems
 
     def copy(to_box, to_dir, chunk, sem):
@@ -95,6 +95,43 @@
         act()
     else:
         pl.when(condition)(act)
+
+
+def exchange(lv, nd, b, d, send, ext, send_sem, recv_sem):
+    result = []
+    for step in range(1, nd):
+        to = lax.rem(d + step, nd)
+        result.append(
+            pltpu.make_async_remote_copy(
+                src_ref=send.at[to],
+                dst_ref=ext.at[lv.halo + d],
+                send_sem=send_sem.at[step],
+                recv_sem=recv_sem.at[nd - step],
+                device_id=(b, to),
+                device_id_type=MESH,
+            )
+        )
+    return result
+
+
+def halo_copies(lv, nd, nb, b, d, ext, sem):
+    up = pltpu.make_async_remote_copy(
+        src_ref=ext.at[pl.ds(nd, lv.halo)],
+        dst_ref=ext.at[pl.ds(0, lv.halo)],
+        send_sem=sem.at[0],
+        recv_sem=sem.at[1],
+        device_id=(b + 1, d),
+        device_id_type=MESH,
+    )
+    down = pltpu.make_async_remote_copy(
+        src_ref=ext.at[pl.ds(lv.halo, lv.halo)],
+        dst_ref=ext.at[pl.ds(lv.halo + nd, lv.halo)],
+        send_sem=sem.at[2],
+        recv_sem=sem.at[3],
+        device_id=(b - 1, d),
+        device_id_type=MESH,
+    )
+    return [(b < nb - 1, b > 0, up), (b > 0, b < nb - 1, down)]
 
 
 def hot_pieces(lv, b, j, sources, targets, op_ids, left, right):
@@ -228,6 +265,7 @@
         (dens1, oper1, bal1, src1, tgt1, ids1, out1),
         (dens2, oper2, bal2, src2, tgt2, ids2, out2),
     )
+    fine_slots = levels[0].slots
     b, d = lax.axis_index("box"), lax.axis_index("dir")
 
     firsts = []
@@ -264,21 +302,18 @@
 
     sides = 1 + (b > 0).astype(jnp.int32) + (b < nb - 1).astype(jnp.int32)
     pl.semaphore_wait(barrier, sides * nd - 1)
-
-    plans = []
+    fine, coarse = levels
+    s = sets[0]
+    sends, receives = direct_copies(fine, nd, nb, b, d, s[1], s[2], (s[9], s[10]))
+    for condition, make in sends:
+        under(condition, lambda make=make: make().start())
+    s = sets[1]
+    swaps = exchange(coarse, nd, b, d, s[1], s[2], s[9], s[10])
+    for swap in swaps:
+        swap.start()
+    halos = halo_copies(coarse, nd, nb, b, d, s[2], s[19])
     for lv, s in zip(levels, sets):
-        send, ext = s[1], s[2]
-        sends, receives = copies(lv, nd, nb, b, d, send, ext, (s[9], s[10]))
-        plans.append((sends, receives))
-        for condition, make in sends:
-            under(condition, lambda make=make: make().start())
-
-    jobs = []
-    for lv, s, waits in zip(levels, sets, firsts):
-        src, tgt, ids = s[15:18]
-        send, ext, lefts, rights, counts = s[1], s[2], s[4], s[5], s[6]
-        for wait in waits[1:]:
-            wait.wait()
+        send, ext, table = s[1], s[2], s[8]
         ext[lv.halo + d] = send[d]
         blank = jnp.zeros(ext.shape[1:], BF16)
 
@@ -292,11 +327,17 @@
             for i in range(lv.halo):
                 ext[lv.halo + nd + i] = blank
 
-        table = s[8]
         hole = jnp.zeros((lv.wide - lv.channel, lv.wide), BF16)
         for parity in range(2):
             for k in range(lv.ops // 2):
                 table[parity, k * lv.wide + lv.channel : (k + 1) * lv.wide, :] = hole
+
+    jobs = []
+    for lv, s, waits in zip(levels, sets, firsts):
+        src, tgt, ids = s[15:18]
+        lefts, rights, counts = s[4], s[5], s[6]
+        for wait in waits[1:]:
+            wait.wait()
         for j in range(lv.slots):
             left, right = lefts.at[j % 2], rights.at[j % 2]
             jobs.append(
@@ -305,16 +346,33 @@
                     functools.partial(count_pieces, lv, j, left, right, counts),
                 )
             )
-
     for act in jobs[0][0]():
         act()
+
+    def hand_halos():
+        for swap in swaps:
+            swap.wait_recv()
+        for gives, _, copy in halos:
+            pl.when(gives)(copy.start)
+
+    def wait_fine():
+        for condition, make in receives:
+            under(condition, lambda make=make: make().wait_recv())
+
+    def wait_coarse():
+        for _, takes, copy in halos:
+            pl.when(takes)(copy.wait_recv)
+
     for i, (_, count) in enumerate(jobs):
         interleave(jobs[i + 1][0]() if i + 1 < len(jobs) else [], count())
+        if i == fine_slots:
+            hand_halos()
 
     results = []
-    for lv, (*_, out), s, (_, receives), loads in zip(levels, data, sets, plans, tables):
-        for condition, make in receives:
-            under(condition, lambda make=make: make().wait_recv())
+    for lv, (*_, out), s, loads, arrive in zip(
+        levels, data, sets, tables, (wait_fine, wait_coarse)
+    ):
+        arrive()
         for load in loads:
             load.wait()
         gather_rows(lv, s[2], s[3], s[7])
@@ -323,9 +381,12 @@
         results.append(pltpu.make_async_copy(s[18], out, s[13].at[4]))
         results[-1].start()
 
-    for sends, receives in plans:
-        for condition, make in sends:
-            under(condition, lambda make=make: make().wait_send())
+    for condition, make in sends:
+        under(condition, lambda make=make: make().wait_send())
+    for swap in swaps:
+        swap.wait_send()
+    for gives, _, copy in halos:
+        pl.when(gives)(copy.wait_send)
     for result in results:
         result.wait()
 
@@ -358,6 +419,7 @@
         pltpu.VMEM((lv.slots, lv.pairs), jnp.int32),
         pltpu.VMEM((lv.slots, lv.pairs), jnp.int32),
         pltpu.VMEM((lv.targets, width), BF16),
+        pltpu.SemaphoreType.DMA((4,)),
     ]
 
 

time: 16.7 us -> 18.9 us (1.13)
  Pallas kernels: 15.8 us -> 18.1 us
    pallas_call x1, Pallas kernels: 14.2 us -> 16.5 us  [per_device(): pl.pallas_call(functools.partial(kernel, levels, nd, nb), out_shape=shape...]
where the time goes in v5:
time: 18.9 us; the launch traced here: 18.8 us
  Pallas kernels  18.1 us (96%)
  between operations  0.64 us (3%)
    pallas_call x1, Pallas kernels, per_device(): pl.pallas_call(functools.partial(kernel, levels, nd, nb), out_shape=shape...  16.5 us
    pallas_call x1, Pallas kernels, per_device(): pl.pallas_call(hand_on, out_shape=shapes, compiler_params=pltpu.CompilerP...  1.62 us

profile of v5, /device:TPU:1, one launch (start us, length us, event | category | flops | bytes accessed | tf_op | source)
XLA Modules:
  0.0 18.8 jit_solution(5304085136061738398)
XLA Ops:
  0.6 16.5 %translate.1 = (bf16[128,384]{1,0:T(8,128)(2,1)}, bf16[64,768]{1,0:T(8,128)(2,1)}) custom-call(bf16[32,1536]{1,0:T(8,128)(2,1)} %refs_0_.1, bf16[16,3072]{1,0:T(8,128)(2,1)} %refs_1_.1, bf16[192,3072]{1,0:T(8,128)(2,1)} %refs_2_.1, bf16[192,3072]{1,0:T(8,128)(2,1)} %refs_3_.1, s32[8]{0:T(128)} %refs_4_.1, s32[16]{0:T(128)} %refs_5_.1, s32[2,2048]{1,0:T(2,128)} %refs_6_.1, ...), custom_call_target="tpu_custom_call" | custom-call | tf_op jit(solution)/shard_map/translate/pallas_call | solution.py:435
  17.2 1.6 %hand_on.1 = (bf16[128,384]{1,0:T(8,128)(2,1)}, bf16[64,768]{1,0:T(8,128)(2,1)}) custom-call(bf16[128,384]{1,0:T(8,128)(2,1)} %get-tuple-element.4.one, bf16[64,768]{1,0:T(8,128)(2,1)} %get-tuple-element.5.two), custom_call_target="tpu_custom_call" | custom-call | tf_op jit(solution)/shard_map/hand_on/pallas_call | solution.py:446

commit v6 on v3

--- a/solution.py
+++ b/solution.py
@@ -252,26 +252,42 @@
         for to in range(nd):
             pl.semaphore_signal(barrier, inc=1, device_id=(b + 1, to), device_id_type=MESH)
 
-    tables = []
-    for lv, (_, oper, *_), s in zip(levels, data, sets):
-        tables.append(operator_copies(lv, oper, s[8], s[11]))
-        for load in tables[-1]:
-            load.start()
-
-    for lv, (_, _, bal, *_), s, first in zip(levels, data, sets, firsts):
+    for lv, s in zip(levels, sets):
+        ext, table = s[2], s[8]
+        blank = jnp.zeros(ext.shape[1:], BF16)
+
+        @pl.when(b == 0)
+        def _():
+            for i in range(lv.halo):
+                ext[i] = blank
+
+        @pl.when(b == nb - 1)
+        def _():
+            for i in range(lv.halo):
+                ext[lv.halo + nd + i] = blank
+
+        hole = jnp.zeros((lv.wide - lv.channel, lv.wide), BF16)
+        for parity in range(2):
+            for k in range(lv.ops // 2):
+                table[parity, k * lv.wide + lv.channel : (k + 1) * lv.wide, :] = hole
+
+    plans = []
+    for at, (lv, (_, _, bal, *_), s, first) in enumerate(zip(levels, data, sets, firsts)):
         first[0].wait()
         sort_slots(lv, nd, s[14], bal, s[0], s[1])
-
-    sides = 1 + (b > 0).astype(jnp.int32) + (b < nb - 1).astype(jnp.int32)
-    pl.semaphore_wait(barrier, sides * nd - 1)
-
-    plans = []
-    for lv, s in zip(levels, sets):
+        if at == 0:
+            sides = 1 + (b > 0).astype(jnp.int32) + (b < nb - 1).astype(jnp.int32)
+            pl.semaphore_wait(barrier, sides * nd - 1)
         send, ext = s[1], s[2]
         sends, receives = copies(lv, nd, nb, b, d, send, ext, (s[9], s[10]))
         plans.append((sends, receives))
         for condition, make in sends:
             under(condition, lambda make=make: make().start())
+    tables = []
+    for lv, (_, oper, *_), s in zip(levels, data, sets):
+        tables.append(operator_copies(lv, oper, s[8], s[11]))
+    for load in tables[0]:
+        load.start()
 
     jobs = []
     for lv, s, waits in zip(levels, sets, firsts):
@@ -280,23 +296,6 @@
         for wait in waits[1:]:
             wait.wait()
         ext[lv.halo + d] = send[d]
-        blank = jnp.zeros(ext.shape[1:], BF16)
-
-        @pl.when(b == 0)
-        def _():
-            for i in range(lv.halo):
-                ext[i] = blank
-
-        @pl.when(b == nb - 1)
-        def _():
-            for i in range(lv.halo):
-                ext[lv.halo + nd + i] = blank
-
-        table = s[8]
-        hole = jnp.zeros((lv.wide - lv.channel, lv.wide), BF16)
-        for parity in range(2):
-            for k in range(lv.ops // 2):
-                table[parity, k * lv.wide + lv.channel : (k + 1) * lv.wide, :] = hole
         for j in range(lv.slots):
             left, right = lefts.at[j % 2], rights.at[j % 2]
             jobs.append(
@@ -310,6 +309,9 @@
         act()
     for i, (_, count) in enumerate(jobs):
         interleave(jobs[i + 1][0]() if i + 1 < len(jobs) else [], count())
+        if i == 0:
+            for load in tables[1]:
+                load.start()
 
     results = []
     for lv, (*_, out), s, (_, receives), loads in zip(levels, data, sets, plans, tables):

time: 16.7 us -> 16.7 us (level)
  no operation moved by 1% of the time
where the time goes in v6:
time: 16.7 us; the launch traced here: 16.5 us
  Pallas kernels  15.9 us (95%)
  between operations  0.64 us (4%)
    pallas_call x1, Pallas kernels, per_device(): pl.pallas_call(functools.partial(kernel, levels, nd, nb), out_shape=shape...  14.3 us
    pallas_call x1, Pallas kernels, per_device(): pl.pallas_call(hand_on, out_shape=shapes, compiler_params=pltpu.CompilerP...  1.62 us

profile of v6, /device:TPU:1, one launch (start us, length us, event | category | flops | bytes accessed | tf_op | source)
XLA Modules:
  0.0 16.5 jit_solution(18319018489833131066)
XLA Ops:
  0.6 14.3 %translate.1 = (bf16[128,384]{1,0:T(8,128)(2,1)}, bf16[64,768]{1,0:T(8,128)(2,1)}) custom-call(bf16[32,1536]{1,0:T(8,128)(2,1)} %refs_0_.1, bf16[16,3072]{1,0:T(8,128)(2,1)} %refs_1_.1, bf16[192,3072]{1,0:T(8,128)(2,1)} %refs_2_.1, bf16[192,3072]{1,0:T(8,128)(2,1)} %refs_3_.1, s32[8]{0:T(128)} %refs_4_.1, s32[16]{0:T(128)} %refs_5_.1, s32[2,2048]{1,0:T(2,128)} %refs_6_.1, ...), custom_call_target="tpu_custom_call" | custom-call | tf_op jit(solution)/shard_map/translate/pallas_call | solution.py:375
  14.9 1.6 %hand_on.1 = (bf16[128,384]{1,0:T(8,128)(2,1)}, bf16[64,768]{1,0:T(8,128)(2,1)}) custom-call(bf16[128,384]{1,0:T(8,128)(2,1)} %get-tuple-element.4.one, bf16[64,768]{1,0:T(8,128)(2,1)} %get-tuple-element.5.two), custom_call_target="tpu_custom_call" | custom-call | tf_op jit(solution)/shard_map/hand_on/pallas_call | solution.py:386

commit v7 on v6

--- a/solution.py
+++ b/solution.py
@@ -77,10 +77,11 @@
         to = lax.rem(d + step, nd)
         up = jnp.logical_and(d >= nd - lv.halo, b < nb - 1)
         down = jnp.logical_and(d < lv.halo, b > 0)
-        if step:
-            sends.append((None, functools.partial(copy, b, to, lv.halo + d, step)))
         sends.append((up, functools.partial(copy, b + 1, to, d - (nd - lv.halo), nd + step)))
         sends.append((down, functools.partial(copy, b - 1, to, lv.halo + nd + d, 2 * nd + step)))
+    for step in range(1, nd):
+        to = lax.rem(d + step, nd)
+        sends.append((None, functools.partial(copy, b, to, lv.halo + d, step)))
     for step in range(1, nd):
         chunk = lv.halo + lax.rem(d + step, nd)
         receives.append((None, functools.partial(copy, b, d, chunk, 0)))

time: 16.7 us -> 17.2 us (1.030)
  the two profiles are of different devices: /device:TPU:1 before, /device:TPU:0 now
where the time goes in v7:
time: 17.2 us; the launch traced here: 17 us
  Pallas kernels  16.3 us (95%)
  between operations  0.64 us (4%)
    pallas_call x1, Pallas kernels, per_device(): pl.pallas_call(functools.partial(kernel, levels, nd, nb), out_shape=shape...  14.7 us
    pallas_call x1, Pallas kernels, per_device(): pl.pallas_call(hand_on, out_shape=shapes, compiler_params=pltpu.CompilerP...  1.62 us

profile of v7, /device:TPU:0, one launch (start us, length us, event | category | flops | bytes accessed | tf_op | source)
XLA Modules:
  0.0 17.0 jit_solution(8649641655539655821)
XLA Ops:
  0.6 14.7 %translate.1 = (bf16[128,384]{1,0:T(8,128)(2,1)}, bf16[64,768]{1,0:T(8,128)(2,1)}) custom-call(bf16[32,1536]{1,0:T(8,128)(2,1)} %refs_0_.1, bf16[16,3072]{1,0:T(8,128)(2,1)} %refs_1_.1, bf16[192,3072]{1,0:T(8,128)(2,1)} %refs_2_.1, bf16[192,3072]{1,0:T(8,128)(2,1)} %refs_3_.1, s32[8]{0:T(128)} %refs_4_.1, s32[16]{0:T(128)} %refs_5_.1, s32[2,2048]{1,0:T(2,128)} %refs_6_.1, ...), custom_call_target="tpu_custom_call" | custom-call | tf_op jit(solution)/shard_map/translate/pallas_call | solution.py:376
  15.3 1.6 %hand_on.1 = (bf16[128,384]{1,0:T(8,128)(2,1)}, bf16[64,768]{1,0:T(8,128)(2,1)}) custom-call(bf16[128,384]{1,0:T(8,128)(2,1)} %get-tuple-element.4.one, bf16[64,768]{1,0:T(8,128)(2,1)} %get-tuple-element.5.two), custom_call_target="tpu_custom_call" | custom-call | tf_op jit(solution)/shard_map/hand_on/pallas_call | solution.py:387
